TPU v7x, 768 devices: a whole 4x8x12 slice. The times are simulated.
768 devices in a mesh: ta: 16 (over y_lo, x, core), sa: 48 (over z, y_hi).
Axes of the slice: x: 4, y: 8 (y_hi: 4, y_lo: 2; y = y_hi * 2 + y_lo), z: 12, core: 2. Of those that a mesh axis runs over, the one named last changes fastest.
Arguments:
- operator: bfloat16 [32, 96, 6, 82944], P('ta', 'sa'), may hold values from -0.625 to 0.625
- vectors: bfloat16 [32, 96, 6, 6144], P('ta', 'sa'), may hold values from -2.5 to 2.5
- aggregate: int32 [6], replicated, may hold values from 0 to 1, as said below
Outputs:
- within_cell: float32 [16, 48, 3, 2, 2, 4096], P('ta', 'sa')
- cross_links: float32 [16, 48, 4, 2, 4096], P('ta', 'sa')
Inputs may be any that keep to these rules, and one draw needn't show every extreme that they name: Every aggregate number is taken by exactly 2 * 3 / 2 sites.
All inputs are finite; a program needn't handle non-finite values.
Results may differ from a plain program's by a relative error of at most 0.0029.
Values may be sent and summed in bfloat16 or wider, within the bound.
A program may use at most 64 MiB of HBM per device.

v0:
```python
import jax
import jax.numpy as jnp
import numpy as np
from jax import lax
from jax.sharding import PartitionSpec as P

BLOCK = 96
NULLCOLS = 64
LX = 2
LY = 3
XSPLIT = 8
AGGS = 2


PRECISE = lax.Precision.HIGHEST


def from_behind(value, axis, by):
    peers = lax.axis_size(axis)
    return lax.ppermute(value, axis, [(i, (i + by) % peers) for i in range(peers)])


def padded_2(block, sides, width):
    for axis, dim in sides:
        count = lax.axis_size(axis)
        forward = [(i, i + 1) for i in range(count - 1)]
        forward.append((count - 1, 0))
        backward = [(target, source) for source, target in forward]
        low = lax.ppermute(
            lax.slice_in_dim(block, block.shape[dim] - width, None, axis=dim), axis, forward
        )
        high = lax.ppermute(lax.slice_in_dim(block, 0, width, axis=dim), axis, backward)
        block = jnp.concatenate([low, block, high], axis=dim)
    return block


def neighbour_table():
    places = np.arange(LX * LY)
    first_coord = places // LY
    second_coord = places % LY
    plus_first = (first_coord + 1) % LX * LY + second_coord
    minus_first = (first_coord - 1) % LX * LY + second_coord
    plus_second = first_coord * LY + (second_coord + 1) % LY
    minus_second = first_coord * LY + (second_coord - 1) % LY
    return np.stack(
        [places, places, places, places, places, plus_first, minus_first, plus_second, minus_second]
    )


def pass_face(plane, offset):
    return from_behind(plane, "sa", offset)


def pass_time(coarse):
    final_slab = coarse.shape[0] - 1
    arrived = from_behind(coarse[final_slab], "ta", 1)
    return coarse[:final_slab].at[0].add(arrived)


def pass_space(coarse):
    final_slab = coarse.shape[1] - 1
    arrived = from_behind(coarse[:, final_slab], "sa", XSPLIT)
    return coarse[:, :final_slab].at[:, 0].add(arrived)


def per_device(operator, vectors, aggregate):
    site_count = LX * LY
    time_count = vectors.shape[0]
    space_count = vectors.shape[1]
    padded = padded_2(vectors, (("ta", 0),), 1)
    z_below = pass_face(vectors[:, space_count - 1], XSPLIT)
    z_above = pass_face(vectors[:, 0], -XSPLIT)
    lattice = vectors.reshape(time_count, space_count, LX, LY, vectors.shape[-1])
    x_slab = lax.axis_index("sa") % XSPLIT
    x_below = jnp.where(
        x_slab == 0,
        pass_face(lattice[:, :, LX - 1], 1 - XSPLIT),
        pass_face(lattice[:, :, LX - 1], 1),
    )
    x_above = jnp.where(
        x_slab == XSPLIT - 1,
        pass_face(lattice[:, :, 0], XSPLIT - 1),
        pass_face(lattice[:, :, 0], -1),
    )
    z_ext = jnp.concatenate([z_below[:, None], vectors, z_above[:, None]], axis=1)
    x_ext = jnp.concatenate([x_below[:, :, None], lattice, x_above[:, :, None]], axis=2)

    def as_blocks(field):
        return field.reshape(time_count, space_count, site_count, BLOCK, NULLCOLS)

    beside = jnp.stack(
        [
            as_blocks(vectors),
            as_blocks(padded[2:]),
            as_blocks(padded[:-2]),
            as_blocks(z_ext[:, 2:]),
            as_blocks(z_ext[:, :-2]),
            as_blocks(x_ext[:, :, 2:]),
            as_blocks(x_ext[:, :, :-2]),
            as_blocks(jnp.roll(lattice, -1, 3)),
            as_blocks(jnp.roll(lattice, 1, 3)),
        ],
        axis=3,
    )
    weights = operator.reshape(time_count, space_count, site_count, 9, BLOCK, BLOCK)
    images = jnp.einsum(
        "tzsmij,tzsmjk->tzsmik", weights, beside, preferred_element_type=jnp.float32
    ).astype(jnp.bfloat16)
    contrib = jnp.einsum(
        "tzsji,tzsmjk->tzsmik", as_blocks(vectors), images, preferred_element_type=jnp.float32
    )
    member = (aggregate[:, None] == jnp.arange(AGGS, dtype=jnp.int32)[None, :]).astype(jnp.float32)
    target = member[neighbour_table()]
    odd_time = (jnp.arange(time_count, dtype=jnp.int32) % 2).astype(jnp.float32)[:, None]
    odd_space = (jnp.arange(space_count, dtype=jnp.int32) % 2).astype(jnp.float32)[None, :]
    filled_tz = jnp.ones((time_count, space_count), jnp.float32)
    cross_mask = jnp.stack(
        [
            (1.0 - odd_time) * filled_tz,
            odd_time * filled_tz,
            (1.0 - odd_space) * filled_tz,
            odd_space * filled_tz,
        ],
        axis=2,
    )
    shape_all = (time_count, space_count, site_count)
    x_local = jnp.arange(site_count, dtype=jnp.int32) // LY
    x_last = jnp.broadcast_to((x_local == LX - 1).astype(jnp.float32), shape_all)
    x_first = jnp.broadcast_to((x_local == 0).astype(jnp.float32), shape_all)
    filled = jnp.ones(shape_all, jnp.float32)
    blank = jnp.zeros(shape_all, jnp.float32)
    columns = [jnp.broadcast_to(cross_mask[:, :, k][:, :, None], shape_all) for k in range(4)]
    route_same = jnp.stack(
        [
            filled,
            1.0 - columns[0],
            1.0 - columns[1],
            1.0 - columns[2],
            1.0 - columns[3],
            1.0 - x_last,
            1.0 - x_first,
            filled,
            filled,
        ],
        axis=3,
    )
    route_next = jnp.stack([blank, blank, blank, blank, blank, x_last, blank, blank, blank], axis=3)
    route_prior = jnp.stack(
        [blank, blank, blank, blank, blank, blank, x_first, blank, blank], axis=3
    )
    route = jnp.stack([route_same, route_next, route_prior], axis=0)
    group_time = (
        (jnp.arange(time_count, dtype=jnp.int32)[:, None] + 1) // 2
        == jnp.arange(time_count // 2 + 1, dtype=jnp.int32)[None, :]
    ).astype(jnp.float32)
    group_space = (
        (jnp.arange(space_count, dtype=jnp.int32)[:, None] + 1) // 2
        == jnp.arange(space_count // 2 + 1, dtype=jnp.int32)[None, :]
    ).astype(jnp.float32)
    hop_select = (
        jnp.arange(9, dtype=jnp.int32)[:, None] == jnp.arange(4, dtype=jnp.int32)[None, :] + 1
    ).astype(jnp.float32)
    slabs_time = time_count // 2 + 1
    slabs_space = space_count // 2 + 1
    within_coef = jnp.einsum(
        "rtzsm,sa,msb,tp,zq->tzsmpqrab", route, member, target, group_time, group_space
    )
    cross_coef = jnp.einsum(
        "mk,tzk,sa,tp,zq->tzsmpqka", hop_select, cross_mask, member, group_time, group_space
    )
    rows = time_count * space_count * site_count * 9
    coef = jnp.concatenate(
        [
            within_coef.reshape(rows, slabs_time, slabs_space, 3 * AGGS * AGGS),
            cross_coef.reshape(rows, slabs_time, slabs_space, 4 * AGGS),
        ],
        axis=3,
    )
    coef = coef.reshape(rows, slabs_time * slabs_space * (3 * AGGS + 4) * AGGS)
    flat = jnp.dot(
        coef.T,
        contrib.reshape(rows, NULLCOLS * NULLCOLS),
        precision=PRECISE,
        preferred_element_type=jnp.float32,
    )
    coarse = flat.reshape(slabs_time, slabs_space, 3 * AGGS + 4, AGGS, NULLCOLS * NULLCOLS)
    coarse = pass_time(pass_space(coarse))
    within_cell = coarse[:, :, : 3 * AGGS].reshape(
        coarse.shape[:2] + (3, AGGS, AGGS, NULLCOLS * NULLCOLS)
    )
    return (within_cell, coarse[:, :, 3 * AGGS :])


def solution(mesh):
    return jax.shard_map(
        per_device,
        mesh=mesh,
        in_specs=(P("ta", "sa", None, None), P("ta", "sa", None, None), P()),
        out_specs=(P("ta", "sa", None, None, None, None), P("ta", "sa", None, None, None)),
        check_vma=False,
    )
```

profile of v0, /device:TPU:120, one launch (start us, length us, event | category | flops | bytes accessed | tf_op | source)
XLA Modules:
  0.0 167.4 jit_solution(10978748582814887929)
XLA Ops:
  0.7 1.9 %slice_bitcast_fusion.2 = (bf16[2,2,3,6144]{3,1,2,0:T(2,128)(2,1)}, bf16[2,2,3,6144]{3,1,2,0:T(2,128)(2,1)}) fusion(bf16[2,2,2,3,6144]{4,1,3,2,0:T(2,128)(2,1)} %bitcast.101), kind=kLoop, calls=%fused_computation.29 | loop fusion | bytes 589824 | tf_op jit(solution)/shard_map/squeeze | solution.py:77
  2.6 7.6 %collective-permute-start.4 = (bf16[2,2,3,6144]{3,1,2,0:T(2,128)(2,1)}, bf16[2,2,3,6144]{3,1,2,0:T(2,128)(2,1)S(1)}, u32[]{:S(2)}, u32[]{:S(2)}) collective-permute-start(bf16[2,2,3,6144]{3,1,2,0:T(2,128)(2,1)} %get-tuple-element.43), channel_id=1, source_target_pairs={{0,7},{1,8},{2,9},{3,10},{4,11},{5,12},{6,13},{7,14},{8,15},{9,16}... | collective-permute-start | bytes 442376 | tf_op jit(solution)/shard_map/ppermute | solution.py:20
  10.3 3.1 %collective-permute-start.5 = (bf16[2,2,3,6144]{3,1,2,0:T(2,128)(2,1)}, bf16[2,2,3,6144]{3,1,2,0:T(2,128)(2,1)}, u32[]{:S(2)}, u32[]{:S(2)}) collective-permute-start(bf16[2,2,3,6144]{3,1,2,0:T(2,128)(2,1)} %get-tuple-element.43), channel_id=1, source_target_pairs={{0,47},{1,0},{2,1},{3,2},{4,3},{5,4},{6,5},{7,6},{8,7},{9,8},{10,9... | collective-permute-start | bytes 442376 | tf_op jit(solution)/shard_map/ppermute | solution.py:20
  13.4 10.3 %collective-permute-start.6 = (bf16[2,2,3,6144]{3,1,2,0:T(2,128)(2,1)}, bf16[2,2,3,6144]{3,1,2,0:T(2,128)(2,1)}, u32[]{:S(2)}, u32[]{:S(2)}) collective-permute-start(bf16[2,2,3,6144]{3,1,2,0:T(2,128)(2,1)} %get-tuple-element.42), channel_id=1, source_target_pairs={{0,41},{1,42},{2,43},{3,44},{4,45},{5,46},{6,47},{7,0},{8,1},{9,2}... | collective-permute-start | bytes 442376 | tf_op jit(solution)/shard_map/ppermute | solution.py:20
  23.7 1.9 %collective-permute-start.7 = (bf16[2,2,3,6144]{3,1,2,0:T(2,128)(2,1)}, bf16[2,2,3,6144]{3,1,2,0:T(2,128)(2,1)}, u32[]{:S(2)}, u32[]{:S(2)}) collective-permute-start(bf16[2,2,3,6144]{3,1,2,0:T(2,128)(2,1)} %get-tuple-element.42), channel_id=1, source_target_pairs={{0,1},{1,2},{2,3},{3,4},{4,5},{5,6},{6,7},{7,8},{8,9},{9,10},{10,1... | collective-permute-start | bytes 442376 | tf_op jit(solution)/shard_map/ppermute | solution.py:20
  25.6 1.7 %fusion.24 = (bf16[2,1,6,6144]{3,1,2,0:T(2,128)(2,1)S(1)}, bf16[2,1,6,6144]{3,1,2,0:T(2,128)(2,1)S(1)}) fusion(bf16[2,2,6,6144]{3,1,2,0:T(2,128)(2,1)} %param.10), kind=kLoop, calls=%fused_computation.77 | loop fusion | bytes 589824 | tf_op jit(solution)/shard_map/slice | solution.py:71
  27.5 8.4 %collective-permute-start.2 = (bf16[2,6,6144]{2,0,1:T(2,128)(2,1)S(1)}, bf16[2,6,6144]{2,0,1:T(2,128)(2,1)S(1)}, u32[]{:S(2)}, u32[]{:S(2)}) collective-permute-start(bf16[2,6,6144]{2,0,1:T(2,128)(2,1)S(1)} %bitcast.107), channel_id=1, source_target_pairs={{0,40},{1,41},{2,42},{3,43},{4,44},{5,45},{6,46},{7,47},{8,0},{9,1... | collective-permute-start | bytes 442376 | tf_op jit(solution)/shard_map/ppermute | solution.py:20
  35.9 1.9 %fusion.25 = (bf16[1,2,6,6144]{3,1,2,0:T(2,128)(2,1)}, bf16[1,2,6,6144]{3,1,2,0:T(2,128)(2,1)}) fusion(bf16[2,2,6,6144]{3,1,2,0:T(2,128)(2,1)} %param.10), kind=kLoop, calls=%fused_computation.78 | loop fusion | bytes 589824 | tf_op jit(solution)/shard_map/slice | solution.py:30
  37.8 1.3 fusion.23
  46.4 10.5 %reshape.189 = bf16[2,2,6,9,96,96]{5,4,3,1,2,0:T(8,128)(2,1)} reshape(bf16[2,2,6,82944]{3,1,2,0:T(2,128)(2,1)} %param.9) | data formatting | bytes 7962624 | tf_op jit(solution)/shard_map/reshape | solution.py:105
  58.5 1.9 %collective-permute-start.3 = (bf16[2,6,6144]{2,0,1:T(2,128)(2,1)S(1)}, bf16[2,6,6144]{2,0,1:T(2,128)(2,1)S(1)}, u32[]{:S(2)}, u32[]{:S(2)}) collective-permute-start(bf16[2,6,6144]{2,0,1:T(2,128)(2,1)S(1)} %bitcast.109), channel_id=1, source_target_pairs={{0,8},{1,9},{2,10},{3,11},{4,12},{5,13},{6,14},{7,15},{8,16},{9,17... | collective-permute-start | bytes 442376 | tf_op jit(solution)/shard_map/ppermute | solution.py:20
  60.4 3.5 %collective-permute-start = (bf16[1,2,6,6144]{3,1,2,0:T(2,128)(2,1)}, bf16[1,2,6,6144]{3,1,2,0:T(2,128)(2,1)S(1)}, u32[]{:S(2)}, u32[]{:S(2)}) collective-permute-start(bf16[1,2,6,6144]{3,1,2,0:T(2,128)(2,1)} %get-tuple-element.51), channel_id=1, source_target_pairs={{48,0},{96,48},{144,96},{192,144},{240,192},{288,240},{336,288},{3... | collective-permute-start | bytes 442376 | tf_op jit(solution)/shard_map/ppermute | solution.py:32
  63.9 1.1 fusion.17
  65.0 1.9 %collective-permute-start.1 = (bf16[1,2,6,6144]{3,1,2,0:T(2,128)(2,1)}, bf16[1,2,6,6144]{3,1,2,0:T(2,128)(2,1)}, u32[]{:S(2)}, u32[]{:S(2)}) collective-permute-start(bf16[1,2,6,6144]{3,1,2,0:T(2,128)(2,1)} %get-tuple-element.50), channel_id=1, source_target_pairs={{0,48},{48,96},{96,144},{144,192},{192,240},{240,288},{288,336},{3... | collective-permute-start | bytes 442376 | tf_op jit(solution)/shard_map/ppermute | solution.py:29
  66.9 1.1 fusion.18
  68.0 1.5 pad_maximum_fusion
  71.4 2.5 %collective-permute-done.1 = bf16[1,2,6,6144]{3,1,2,0:T(2,128)(2,1)} collective-permute-done((bf16[1,2,6,6144]{3,1,2,0:T(2,128)(2,1)}, bf16[1,2,6,6144]{3,1,2,0:T(2,128)(2,1)}, u32[]{:S(2)}, u32[]{:S(2)}) %collective-permute-start.1) | collective-permute-done | bytes 147488 | tf_op jit(solution)/shard_map/ppermute | solution.py:29
  73.9 3.4 %pad_maximum_fusion.2 = (bf16[2,2,6,6144]{3,1,2,0:T(2,128)(2,1)}, bf16[2,2,6,6144]{3,1,2,0:T(2,128)(2,1)S(1)}, bf16[2,2,6,6144]{3,1,2,0:T(2,128)(2,1)S(1)}, bf16[2,2,6,6144]{3,1,2,0:T(2,128)(2,1)}) fusion(bf16[2,2,6,6144]{3,1,2,0:T(2,128)(2,1)S(1)} %copy-done, bf16[2,1,6,6144]{3,1,2,0:T(2,128)(2,1)S(1)} %copy.107, bf16[1,2,6,6144]{3,1,2,0:T(2,128)(2,1)} %copy-done.3, ...), kind=kLoop, calls=%fused_computation.18 | loop fusion | flops 2359296 | bytes 2064384 | tf_op jit(solution)/shard_map/concatenate | solution.py:85
  78.6 1.4 stack_reshape.30
  80.0 1.0 copy.113
  81.4 1.0 copy.114
  82.4 1.4 stack_reshape.33
  86.5 1.9 %constant_dynamic-update-slice_fusion.5 = bf16[2,2,6,9,96,64]{4,5,3,2,1,0:T(8,128)(2,1)} fusion(bf16[2,2,6,9,96,64]{4,5,3,2,1,0:T(8,128)(2,1)} %constant_dynamic-update-slice_fusion.6, bf16[2,2,6,1,96,64]{4,5,3,2,1,0:T(8,128)(2,1)} %copy.113), kind=kLoop, calls=%fused_computation.42 | loop fusion | bytes 786432
  88.3 1.8 %constant_dynamic-update-slice_fusion.4 = bf16[2,2,6,9,96,64]{4,5,3,2,1,0:T(8,128)(2,1)} fusion(bf16[2,2,6,9,96,64]{4,5,3,2,1,0:T(8,128)(2,1)} %constant_dynamic-update-slice_fusion.5, bf16[2,2,6,1,96,64]{4,5,3,2,1,0:T(8,128)(2,1)} %copy.114), kind=kLoop, calls=%fused_computation.41 | loop fusion | bytes 786432
  93.6 8.1 %fusion.11 = f32[2,2,6,9,64,64]{4,5,3,2,1,0:T(8,128)} fusion(bf16[2,2,6,9,96,64]{4,5,3,2,1,0:T(8,128)(2,1)} %constant_dynamic-update-slice_fusion, bf16[2,2,6,9,96,96]{5,4,3,1,2,0:T(8,128)(2,1)} %reshape.189, bf16[2,2,6,96,64]{4,3,1,2,0:T(8,128)(2,1)S(1)} %reshape.190), kind=kOutput, calls=%fused_computation.8 | convolution fusion | flops 426000384 | bytes 10469376 | tf_op jit(solution)/shard_map/tzsji,tzsmjk->tzsmik/dot_general | solution.py:109
  101.7 8.0 %copy.121 = f32[2,2,6,9,64,64]{5,4,3,2,1,0:T(8,128)} copy(f32[2,2,6,9,64,64]{4,5,3,2,1,0:T(8,128)} %fusion.11) | data formatting | bytes 7077888 | tf_op jit(solution)/shard_map/tzsji,tzsmjk->tzsmik/transpose | solution.py:109
  109.7 6.9 %reshape.206 = f32[216,4096,1,1,1]{1,0,2,3,4:T(8,128)} reshape(f32[2,2,6,9,64,64]{5,4,3,2,1,0:T(8,128)} %copy.121) | data formatting | bytes 7077888 | tf_op jit(solution)/shard_map/reshape | solution.py:182
  116.6 4.1 %fusion.2 = f32[2,2,10,2,4096]{4,2,3,1,0:T(8,128)S(1)} fusion(f32[216,4096,1,1,1]{1,0,2,3,4:T(8,128)} %reshape.206, f32[2,2,10,2,216]{4,3,2,1,0:T(2,128)S(1)} %dot_general.97), kind=kOutput, calls=%fused_computation.3 | convolution fusion | flops 849346560 | bytes 4918784 | tf_op jit(solution)/shard_map/dot_general | solution.py:180
  121.3 1.9 %collective-permute-start.8 = (f32[2,10,2,4096]{3,2,1,0:T(2,128)S(1)}, f32[2,10,2,4096]{3,2,1,0:T(2,128)S(1)}, u32[]{:S(2)}, u32[]{:S(2)}) collective-permute-start(f32[2,10,2,4096]{3,2,1,0:T(2,128)S(1)} %copy.123), channel_id=1, source_target_pairs={{0,8},{1,9},{2,10},{3,11},{4,12},{5,13},{6,14},{7,15},{8,16},{9,17... | collective-permute-start | bytes 1966088 | tf_op jit(solution)/shard_map/ppermute | solution.py:20
  123.3 29.3 %collective-permute-done.8 = f32[2,10,2,4096]{3,2,1,0:T(2,128)S(1)} collective-permute-done((f32[2,10,2,4096]{3,2,1,0:T(2,128)S(1)}, f32[2,10,2,4096]{3,2,1,0:T(2,128)S(1)}, u32[]{:S(2)}, u32[]{:S(2)}) %collective-permute-start.8) | collective-permute-done | bytes 655392 | tf_op jit(solution)/shard_map/ppermute | solution.py:20
  153.1 1.9 %collective-permute-start.9 = (f32[1,10,2,4096]{3,1,2,0:T(8,128)S(1)}, f32[1,10,2,4096]{3,1,2,0:T(8,128)S(1)}, u32[]{:S(2)}, u32[]{:S(2)}) collective-permute-start(f32[1,10,2,4096]{3,1,2,0:T(8,128)S(1)} %slice_bitcast_fusion.1), channel_id=1, source_target_pairs={{0,48},{48,96},{96,144},{144,192},{192,240},{240,288},{288,336},{3... | collective-permute-start | bytes 983048 | tf_op jit(solution)/shard_map/ppermute | solution.py:20
  155.0 10.7 %collective-permute-done.9 = f32[1,10,2,4096]{3,1,2,0:T(8,128)S(1)} collective-permute-done((f32[1,10,2,4096]{3,1,2,0:T(8,128)S(1)}, f32[1,10,2,4096]{3,1,2,0:T(8,128)S(1)}, u32[]{:S(2)}, u32[]{:S(2)}) %collective-permute-start.9) | collective-permute-done | bytes 327712 | tf_op jit(solution)/shard_map/ppermute | solution.py:20
  (114 shorter events, 21.2 us)
Async XLA Ops:
  0.6 40.0 %copy-start.5 = (s32[54]{0:T(128)S(1)}, s32[54]{0:T(128)}, u32[]{:S(2)}) copy-start(s32[54]{0:T(128)} %constant.131) | copy-start | bytes 652
  0.6 38.5 %copy-start = (bf16[2,2,6,6144]{3,1,2,0:T(2,128)(2,1)S(1)}, bf16[2,2,6,6144]{3,1,2,0:T(2,128)(2,1)}, u32[]{:S(2)}) copy-start(bf16[2,2,6,6144]{3,1,2,0:T(2,128)(2,1)} %param.10) | copy-start | bytes 884740
  0.7 39.8 %copy-start.6 = (s32[6]{0:T(128)S(1)}, s32[6]{0:T(128)}, u32[]{:S(2)}) copy-start(s32[6]{0:T(128)} %param.11) | copy-start | bytes 76
  2.6 55.2 %collective-permute-start.4 = (bf16[2,2,3,6144]{3,1,2,0:T(2,128)(2,1)}, bf16[2,2,3,6144]{3,1,2,0:T(2,128)(2,1)S(1)}, u32[]{:S(2)}, u32[]{:S(2)}) collective-permute-start(bf16[2,2,3,6144]{3,1,2,0:T(2,128)(2,1)} %get-tuple-element.43), channel_id=1, source_target_pairs={{0,7},{1,8},{2,9},{3,10},{4,11},{5,12},{6,13},{7,14},{8,15},{9,16}... | collective-permute-start | bytes 442376 | tf_op jit(solution)/shard_map/ppermute | solution.py:20
  10.3 50.1 %collective-permute-start.5 = (bf16[2,2,3,6144]{3,1,2,0:T(2,128)(2,1)}, bf16[2,2,3,6144]{3,1,2,0:T(2,128)(2,1)}, u32[]{:S(2)}, u32[]{:S(2)}) collective-permute-start(bf16[2,2,3,6144]{3,1,2,0:T(2,128)(2,1)} %get-tuple-element.43), channel_id=1, source_target_pairs={{0,47},{1,0},{2,1},{3,2},{4,3},{5,4},{6,5},{7,6},{8,7},{9,8},{10,9... | collective-permute-start | bytes 442376 | tf_op jit(solution)/shard_map/ppermute | solution.py:20
  13.4 51.6 %collective-permute-start.6 = (bf16[2,2,3,6144]{3,1,2,0:T(2,128)(2,1)}, bf16[2,2,3,6144]{3,1,2,0:T(2,128)(2,1)}, u32[]{:S(2)}, u32[]{:S(2)}) collective-permute-start(bf16[2,2,3,6144]{3,1,2,0:T(2,128)(2,1)} %get-tuple-element.42), channel_id=1, source_target_pairs={{0,41},{1,42},{2,43},{3,44},{4,45},{5,46},{6,47},{7,0},{8,1},{9,2}... | collective-permute-start | bytes 442376 | tf_op jit(solution)/shard_map/ppermute | solution.py:20
  23.7 43.2 %collective-permute-start.7 = (bf16[2,2,3,6144]{3,1,2,0:T(2,128)(2,1)}, bf16[2,2,3,6144]{3,1,2,0:T(2,128)(2,1)}, u32[]{:S(2)}, u32[]{:S(2)}) collective-permute-start(bf16[2,2,3,6144]{3,1,2,0:T(2,128)(2,1)} %get-tuple-element.42), channel_id=1, source_target_pairs={{0,1},{1,2},{2,3},{3,4},{4,5},{5,6},{6,7},{7,8},{8,9},{9,10},{10,1... | collective-permute-start | bytes 442376 | tf_op jit(solution)/shard_map/ppermute | solution.py:20
  27.5 42.7 %collective-permute-start.2 = (bf16[2,6,6144]{2,0,1:T(2,128)(2,1)S(1)}, bf16[2,6,6144]{2,0,1:T(2,128)(2,1)S(1)}, u32[]{:S(2)}, u32[]{:S(2)}) collective-permute-start(bf16[2,6,6144]{2,0,1:T(2,128)(2,1)S(1)} %bitcast.107), channel_id=1, source_target_pairs={{0,40},{1,41},{2,42},{3,43},{4,44},{5,45},{6,46},{7,47},{8,0},{9,1... | collective-permute-start | bytes 442376 | tf_op jit(solution)/shard_map/ppermute | solution.py:20
  57.8 0.7 copy-start.4
  58.5 12.0 %collective-permute-start.3 = (bf16[2,6,6144]{2,0,1:T(2,128)(2,1)S(1)}, bf16[2,6,6144]{2,0,1:T(2,128)(2,1)S(1)}, u32[]{:S(2)}, u32[]{:S(2)}) collective-permute-start(bf16[2,6,6144]{2,0,1:T(2,128)(2,1)S(1)} %bitcast.109), channel_id=1, source_target_pairs={{0,8},{1,9},{2,10},{3,11},{4,12},{5,13},{6,14},{7,15},{8,16},{9,17... | collective-permute-start | bytes 442376 | tf_op jit(solution)/shard_map/ppermute | solution.py:20
  60.4 10.3 %collective-permute-start = (bf16[1,2,6,6144]{3,1,2,0:T(2,128)(2,1)}, bf16[1,2,6,6144]{3,1,2,0:T(2,128)(2,1)S(1)}, u32[]{:S(2)}, u32[]{:S(2)}) collective-permute-start(bf16[1,2,6,6144]{3,1,2,0:T(2,128)(2,1)} %get-tuple-element.51), channel_id=1, source_target_pairs={{48,0},{96,48},{144,96},{192,144},{240,192},{288,240},{336,288},{3... | collective-permute-start | bytes 442376 | tf_op jit(solution)/shard_map/ppermute | solution.py:32
  65.0 8.9 %collective-permute-start.1 = (bf16[1,2,6,6144]{3,1,2,0:T(2,128)(2,1)}, bf16[1,2,6,6144]{3,1,2,0:T(2,128)(2,1)}, u32[]{:S(2)}, u32[]{:S(2)}) collective-permute-start(bf16[1,2,6,6144]{3,1,2,0:T(2,128)(2,1)} %get-tuple-element.50), channel_id=1, source_target_pairs={{0,48},{48,96},{96,144},{144,192},{192,240},{240,288},{288,336},{3... | collective-permute-start | bytes 442376 | tf_op jit(solution)/shard_map/ppermute | solution.py:29
  70.7 0.7 copy-start.3
  77.3 3.7 %copy-start.2 = (bf16[2,2,6,6144]{3,1,2,0:T(2,128)(2,1)S(1)}, bf16[2,2,6,6144]{3,1,2,0:T(2,128)(2,1)}, u32[]{:S(2)}) copy-start(bf16[2,2,6,6144]{3,1,2,0:T(2,128)(2,1)} %get-tuple-element.44) | copy-start | bytes 884740
  84.7 6.3 %copy-start.1 = (bf16[2,2,6,1,96,64]{4,5,3,2,1,0:T(8,128)(2,1)S(1)}, bf16[2,2,6,1,96,64]{4,5,3,2,1,0:T(8,128)(2,1)}, u32[]{:S(2)}) copy-start(bf16[2,2,6,1,96,64]{4,5,3,2,1,0:T(8,128)(2,1)} %copy.116) | copy-start | bytes 884740
  121.3 31.3 %collective-permute-start.8 = (f32[2,10,2,4096]{3,2,1,0:T(2,128)S(1)}, f32[2,10,2,4096]{3,2,1,0:T(2,128)S(1)}, u32[]{:S(2)}, u32[]{:S(2)}) collective-permute-start(f32[2,10,2,4096]{3,2,1,0:T(2,128)S(1)} %copy.123), channel_id=1, source_target_pairs={{0,8},{1,9},{2,10},{3,11},{4,12},{5,13},{6,14},{7,15},{8,16},{9,17... | collective-permute-start | bytes 1966088 | tf_op jit(solution)/shard_map/ppermute | solution.py:20
  153.1 12.6 %collective-permute-start.9 = (f32[1,10,2,4096]{3,1,2,0:T(8,128)S(1)}, f32[1,10,2,4096]{3,1,2,0:T(8,128)S(1)}, u32[]{:S(2)}, u32[]{:S(2)}) collective-permute-start(f32[1,10,2,4096]{3,1,2,0:T(8,128)S(1)} %slice_bitcast_fusion.1), channel_id=1, source_target_pairs={{0,48},{48,96},{96,144},{144,192},{192,240},{240,288},{288,336},{3... | collective-permute-start | bytes 983048 | tf_op jit(solution)/shard_map/ppermute | solution.py:20
where the time goes:
time: 169 us; the launch traced here: 167 us
  local copies, waits for them, and re-layouts  59.4 us (35%)
  starting transfers between devices  42.5 us (25%)
  waiting for transfers between devices  42.5 us (25%)
  matrix products  12.3 us (7%)
  other arithmetic  9.46 us (6%)
    ppermute x8, waiting for transfers between devices, from_behind(): lax.ppermute(value, axis, [(i, (i + by) % peers) for i in range(peers)])  40 us
    ppermute x8, starting transfers between devices, from_behind(): lax.ppermute(value, axis, [(i, (i + by) % peers) for i in range(peers)])  37.1 us
    unnamed x23, local copies, waits for them, and re-layouts  10.9 us
    another operation x19, local copies, waits for them, and re-layouts, per_device(): jnp.stack([as_blocks(vectors), as_blocks(padded[2:]), as_blocks(padded[:-...  10.8 us
    reshape x1, local copies, waits for them, and re-layouts, per_device(): operator.reshape(time_count, space_count, site_count, 9, BLOCK, BLOCK)  10.5 us
    dot_general x1, matrix products, per_device(): jnp.einsum('tzsji,tzsmjk->tzsmik', as_blocks(vectors), images, preferred_...  8.14 us
    transpose x1, local copies, waits for them, and re-layouts, per_device(): jnp.einsum('tzsji,tzsmjk->tzsmik', as_blocks(vectors), images, preferred_...  8.01 us
    reshape x1, local copies, waits for them, and re-layouts, per_device(): contrib.reshape(rows, NULLCOLS * NULLCOLS)  6.87 us
  transfers between devices with their start and end apart: 10, of which 3 were waited for; matrix products, arithmetic and copies ran while one was open for 17% of the time, Pallas kernels for 0%

commit v1 on v0

v1 whole, which is shorter than its diff:
```python
import jax
import jax.numpy as jnp
from jax import lax
from jax.experimental import pallas as pl
from jax.experimental.pallas import tpu as pltpu
from jax.sharding import PartitionSpec as P

BLOCK = 96
NULLCOLS = 64
LX = 2
LY = 3
XSPLIT = 8
AGGS = 2
SITES = LX * LY
HOPS = 9
LANES = 128
GROUPS = BLOCK // 4
MESH = pl.DeviceIdType.MESH
F32 = jnp.float32
BF16 = jnp.bfloat16


def lane_half(rows):
    return lax.broadcasted_iota(jnp.int32, (rows, LANES), 1) < NULLCOLS


def swap(value):
    return pltpu.roll(value, NULLCOLS, 1)


def block_weights(packed):
    low = lane_half(BLOCK)
    wide = packed.astype(F32)
    turned = swap(wide)
    zero = jnp.zeros_like(wide)
    gap = jnp.zeros((2 * LANES - 2 * BLOCK, LANES), BF16)
    out = []
    for first, second in ((wide, turned), (turned, wide)):
        left = jnp.where(low, first, zero).astype(BF16)
        right = jnp.where(low, zero, second).astype(BF16)
        out.append((jnp.concatenate([left, right, gap], axis=0), jnp.concatenate([gap, left, right], axis=0)))
    return out


def kernel(
    agg_ref, op_hbm, vec_hbm, within_ref, cross_ref,
    op_v, vec_v, op_f, vec_f, mix, pack_z, pack_x, halo_t, halo_z, halo_x, img, turn, left, rhs,
    part, pt_out, pt_in, pz_out, pz_in, load_sem, send_sem, recv_sem,
):
    nt = lax.axis_size("ta")
    ns = lax.axis_size("sa")
    ti = lax.axis_index("ta")
    sj = lax.axis_index("sa")
    slab = sj // XSPLIT * XSPLIT
    xi = sj % XSPLIT
    t_up = ((ti + 1) % nt, sj)
    t_down = ((ti + nt - 1) % nt, sj)
    z_up = (ti, (sj + XSPLIT) % ns)
    z_down = (ti, (sj + ns - XSPLIT) % ns)
    x_up = (ti, slab + (xi + 1) % XSPLIT)
    x_down = (ti, slab + (xi + XSPLIT - 1) % XSPLIT)

    barrier = pltpu.get_barrier_semaphore()
    for there in (t_up, t_down, z_up, z_down, x_up, x_down):
        pl.semaphore_signal(barrier, inc=1, device_id=there, device_id_type=MESH)
    vec_load = pltpu.make_async_copy(vec_hbm, vec_v, load_sem.at[2])
    vec_load.start()
    op_loads = [pltpu.make_async_copy(op_hbm.at[t], op_v.at[t], load_sem.at[t]) for t in range(2)]
    for load in op_loads:
        load.start()

    def remote(index, src, dst, there):
        return pltpu.make_async_remote_copy(
            src_ref=src, dst_ref=dst, send_sem=send_sem.at[index], recv_sem=recv_sem.at[index],
            device_id=there, device_id_type=MESH,
        )

    vec_load.wait()
    low48 = lane_half(48)

    def vec_site(ts, carry):
        vec_f[ts] = vec_v[ts // SITES, ts % SITES].astype(F32)
        v0 = vec_f[ts, pl.ds(0, 48, stride=2), :]
        v1 = vec_f[ts, pl.ds(1, 48, stride=2), :]
        mix[0, pl.ds(0, 48, stride=2), :] = jnp.where(low48, v0, swap(v1))
        mix[0, pl.ds(1, 48, stride=2), :] = jnp.where(low48, swap(v0), v1)
        pack_z[ts // SITES, ts % SITES] = mix[0].astype(BF16)
        return carry

    lax.fori_loop(0, 2 * SITES, vec_site, 0)

    def vec_pair(tzx, carry):
        t, z, x2 = tzx // 6, tzx // 3 % 2, tzx % 3
        v0 = vec_f[t * SITES + x2, pl.ds(z, 48, stride=2), :]
        v1 = vec_f[t * SITES + LY + x2, pl.ds(z, 48, stride=2), :]
        mix[1, pl.ds(0, 48, stride=2), :] = jnp.where(low48, v0, swap(v1))
        mix[1, pl.ds(1, 48, stride=2), :] = jnp.where(low48, swap(v0), v1)
        pack_x[t, z, x2] = mix[1].astype(BF16)
        return carry

    lax.fori_loop(0, 12, vec_pair, 0)

    pl.semaphore_wait(barrier, 6)
    t_face = {
        1: remote(0, pack_x.at[1], halo_t.at[0], t_up),
        0: remote(1, pack_x.at[0], halo_t.at[1], t_down),
    }
    t_face[1].start()
    t_face[0].start()
    faces = {}
    for t in (1, 0):
        faces[t] = (
            remote(2 + 4 * t, pack_z.at[t, LY:SITES], halo_x.at[0, t], x_up),
            remote(3 + 4 * t, pack_z.at[t, 0:LY], halo_x.at[1, t], x_down),
            remote(4 + 4 * t, pack_x.at[t, 1], halo_z.at[0, t], z_up),
            remote(5 + 4 * t, pack_x.at[t, 0], halo_z.at[1, t], z_down),
        )
        for face in faces[t]:
            face.start()

    for t in range(2):
        op_loads[t].wait()

        def widen(s, carry):
            op_f[t * SITES + s] = op_v[t, s].astype(F32)
            return carry

        lax.fori_loop(0, SITES, widen, 0)

    def rows_of(ts, z, hop):
        return [
            op_f[ts, pl.ds(hop * 144 + 2 * v + z, GROUPS, stride=6), :] for v in range(3)
        ]

    def images(users, weights):
        parts = [rows_of(ts, z, hop) for ts, z, hop in users]
        tiles = [jnp.concatenate([part[v] for part in parts], axis=0).astype(BF16) for v in range(3)]
        for half in range(2):
            got = jnp.dot(
                jnp.concatenate([tiles[half], tiles[half + 1]], axis=1), weights[half],
                preferred_element_type=F32,
            ).astype(BF16).astype(F32)
            for i, (ts, z, hop) in enumerate(users):
                img[ts * 2 + z, hop, :, LANES * half:LANES * (half + 1)] = got[GROUPS * i:GROUPS * (i + 1)]

    def local(tz, carry):
        t, z = tz // 2, tz % 2
        for x2 in range(LY):
            both = block_weights(pack_x[t, z, x2])
            for x1 in range(LX):
                s = x1 * LY + x2
                users = (
                    (t * SITES + s, z, 0),
                    ((1 - t) * SITES + s, z, 2 - t),
                    (t * SITES + s, 1 - z, 4 - z),
                    (t * SITES + (1 - x1) * LY + x2, z, 5 if x1 == 1 else 6),
                    (t * SITES + x1 * LY + (x2 + 2) % LY, z, 7),
                    (t * SITES + x1 * LY + (x2 + 1) % LY, z, 8),
                )
                images(users, both[x1])
        return carry

    lax.fori_loop(0, 4, local, 0)

    column = lax.broadcasted_iota(jnp.int32, (1, SITES * GROUPS), 1)
    member = [agg_ref[s].astype(F32) for s in range(SITES)]
    others = [1.0 - m for m in member]
    weight_of = (others, member)
    mask = []
    for a in range(AGGS):
        row = jnp.zeros((1, SITES * GROUPS), F32)
        for s in range(SITES):
            inside = jnp.logical_and(column >= s * GROUPS, column < (s + 1) * GROUPS)
            row = row + jnp.where(inside, weight_of[a][s], 0.0)
        mask.append(row)
    pad = jnp.zeros((2 * LANES - SITES * GROUPS, LANES), F32)

    def left_side(tz, carry):
        t, z = tz // 2, tz % 2
        for h in range(2):
            blocks = [vec_f[t * SITES + s, pl.ds(2 * h + z, GROUPS, stride=4), :] for s in range(SITES)]
            turned = jnp.transpose(jnp.concatenate(blocks + [pad], axis=0))
            for side in range(2):
                turn[side] = turned[:, LANES * side:LANES * (side + 1)]
            for low in range(2):
                for par in range(2):
                    rows = jnp.concatenate(
                        [turn[side, pl.ds(low * NULLCOLS + par, 32, stride=2), :] for side in range(2)], axis=1
                    )[:, :SITES * GROUPS]
                    for a in range(AGGS):
                        at = ((a * 2 + low) * 2 + par) * 32
                        left[tz, h, at:at + 32, :] = (rows * mask[a]).astype(BF16)
        return carry

    lax.fori_loop(0, 4, left_side, 0)

    def halo(t):
        def below_above(zx, carry):
            z, x2 = zx // LY, zx % LY
            both = block_weights(halo_t[t, z, x2])
            for x1 in range(LX):
                images(((t * SITES + x1 * LY + x2, z, 2 - t),), both[x1])
            return carry

        def z_side(zx, carry):
            z, x2 = zx // LY, zx % LY
            both = block_weights(halo_z[z, t, x2])
            for x1 in range(LX):
                images(((t * SITES + x1 * LY + x2, z, 4 - z),), both[x1])
            return carry

        def x_side(s, carry):
            x1, x2 = s // LY, s % LY
            both = block_weights(halo_x[x1, t, x2])
            for z in range(2):
                images(((t * SITES + s, z, 6 - x1),), both[z])
            return carry

        return below_above, z_side, x_side

    low32 = lane_half(32)

    def quarter(t, z, keep):
        tz = t * 2 + z
        t_stay, t_leave = (1, 2) if t == 1 else (2, 1)
        z_stay, z_leave = (3, 4) if z == 1 else (4, 3)
        for h in range(2):
            cut = slice(LANES * h, LANES * (h + 1))
            columns = [[] for _ in range(8)]
            blank = jnp.zeros((GROUPS, LANES), F32)
            for s in range(SITES):
                x1, x2 = s // LY, s % LY
                at = (t * SITES + s) * 2 + z
                take = lambda hop: img[at, hop, :, cut]
                same = take(0) + take(t_stay) + take(z_stay)
                x_stay, x_leave = (6, 5) if x1 == 1 else (5, 6)
                across = (1 - x1) * LY + x2
                up, down = x1 * LY + (x2 + 1) % LY, x1 * LY + (x2 + 2) % LY
                inner, plus, minus, outer = take(x_stay), take(7), take(8), take(x_leave)
                for b in range(AGGS):
                    w = weight_of[b]
                    columns[b].append(w[s] * same + w[across] * inner + w[up] * plus + w[down] * minus)
                    columns[2 + b].append(w[across] * outer if x1 == 1 else blank)
                    columns[4 + b].append(w[across] * outer if x1 == 0 else blank)
                columns[6].append(take(t_leave))
                columns[7].append(take(z_leave))
            for n in range(4):
                rhs[h, n] = jnp.concatenate(
                    [jnp.concatenate(columns[2 * n + c], axis=0).astype(BF16) for c in range(2)], axis=1
                )
        for n in range(4):
            for a in range(AGGS):
                rows = slice(LANES * a, LANES * (a + 1))
                got = jnp.dot(left[tz, 0, rows, :], rhs[0, n], preferred_element_type=F32)
                got = got + jnp.dot(left[tz, 1, rows, :], rhs[1, n], preferred_element_type=F32)
                for c in range(2):
                    cut = got[:, LANES * c:LANES * (c + 1)]
                    value = jnp.where(
                        low32, cut[0:32] + swap(cut[64:96]), swap(cut[32:64]) + cut[96:128]
                    )
                    keep(n * 4 + a * 2 + c if n < 3 else 12 + c * 2 + a, value)

    def send_block(z):
        def keep(block, value):
            pt_out[z, block] = value.astype(BF16)

        return keep

    def keep_block(z):
        def keep(block, value):
            part[z, block] = value

        return keep

    def halo_done(t):
        below_above, z_side, x_side = halo(t)
        t_face[1 - t].wait_recv()
        lax.fori_loop(0, 6, below_above, 0)
        faces[t][0].wait_recv()
        faces[t][1].wait_recv()
        lax.fori_loop(0, 6, x_side, 0)
        faces[t][2].wait_recv()
        faces[t][3].wait_recv()
        lax.fori_loop(0, 6, z_side, 0)

    pt = {z: remote(10 + z, pt_out.at[z], pt_in.at[z], t_up) for z in range(2)}
    pz = remote(12, pz_out, pz_in, z_up)

    halo_done(1)
    quarter(1, 1, send_block(1))
    pt[1].start()
    quarter(1, 0, send_block(0))
    pt[0].start()
    halo_done(0)
    quarter(0, 1, keep_block(1))
    pt[1].wait_recv()
    for block in range(12):
        pz_out[block] = (part[1, block] + pt_in[1, block].astype(F32)).astype(BF16)
    for a in range(AGGS):
        pz_out[12 + a] = part[1, 12 + a].astype(BF16)
        pz_out[14 + a] = pt_in[1, 12 + a]
        pz_out[16 + a] = (part[1, 14 + a] + pt_in[1, 14 + a].astype(F32)).astype(BF16)
    pz.start()
    quarter(0, 0, keep_block(0))
    pt[0].wait_recv()
    for block in range(12):
        part[0, block] = part[0, block] + pt_in[0, block].astype(F32)
    for a in range(AGGS):
        part[0, 14 + a] = part[0, 14 + a] + pt_in[0, 14 + a].astype(F32)
    pz.wait_recv()
    for block in range(12):
        ra, b = block // 2, block % 2
        within_ref[ra, pl.ds(b, 32, stride=2), :] = part[0, block] + pz_in[block].astype(F32)
    for a in range(AGGS):
        cross_ref[0, pl.ds(a, 32, stride=2), :] = part[0, 12 + a] + pz_in[12 + a].astype(F32)
        cross_ref[1, pl.ds(a, 32, stride=2), :] = pt_in[0, 12 + a].astype(F32) + pz_in[14 + a].astype(F32)
        cross_ref[2, pl.ds(a, 32, stride=2), :] = part[0, 14 + a]
        cross_ref[3, pl.ds(a, 32, stride=2), :] = pz_in[16 + a].astype(F32)
    for copy in (t_face[0], t_face[1], *faces[0], *faces[1], pt[0], pt[1], pz):
        copy.wait_send()


def lane_tiles(field):
    time, depth, sites, length = field.shape
    split = field.reshape(time, depth, sites, length // LANES, LANES)
    return split.transpose(0, 2, 3, 1, 4).reshape(time, sites, length // LANES * depth, LANES)


def per_device(operator, vectors, aggregate):
    op_rows = HOPS * BLOCK * BLOCK // LANES * 2
    vec_rows = BLOCK * NULLCOLS // LANES * 2
    within, cross = pl.pallas_call(
        kernel,
        out_shape=(
            jax.ShapeDtypeStruct((3 * AGGS, 64, LANES), F32),
            jax.ShapeDtypeStruct((4, 64, LANES), F32),
        ),
        in_specs=[
            pl.BlockSpec(memory_space=pltpu.SMEM),
            pl.BlockSpec(memory_space=pltpu.HBM),
            pl.BlockSpec(memory_space=pltpu.HBM),
        ],
        out_specs=[pl.BlockSpec(memory_space=pltpu.VMEM)] * 2,
        scratch_shapes=[
            pltpu.VMEM((2, SITES, op_rows, LANES), BF16),
            pltpu.VMEM((2, SITES, vec_rows, LANES), BF16),
            pltpu.VMEM((2 * SITES, op_rows, LANES), F32),
            pltpu.VMEM((2 * SITES, vec_rows, LANES), F32),
            pltpu.VMEM((2, BLOCK, LANES), F32),
            pltpu.VMEM((2, SITES, BLOCK, LANES), BF16),
            pltpu.VMEM((2, 2, LY, BLOCK, LANES), BF16),
            pltpu.VMEM((2, 2, LY, BLOCK, LANES), BF16),
            pltpu.VMEM((2, 2, LY, BLOCK, LANES), BF16),
            pltpu.VMEM((2, 2, LY, BLOCK, LANES), BF16),
            pltpu.VMEM((4 * SITES, HOPS, GROUPS, 2 * LANES), F32),
            pltpu.VMEM((2, LANES, LANES), F32),
            pltpu.VMEM((4, 2, 2 * LANES, SITES * GROUPS), BF16),
            pltpu.VMEM((2, 4, SITES * GROUPS, 2 * LANES), BF16),
            pltpu.VMEM((2, 16, 32, LANES), F32),
            pltpu.VMEM((2, 16, 32, LANES), BF16),
            pltpu.VMEM((2, 16, 32, LANES), BF16),
            pltpu.VMEM((18, 32, LANES), BF16),
            pltpu.VMEM((18, 32, LANES), BF16),
            pltpu.SemaphoreType.DMA((3,)),
            pltpu.SemaphoreType.DMA((13,)),
            pltpu.SemaphoreType.DMA((13,)),
        ],
        compiler_params=pltpu.CompilerParams(
            collective_id=0, has_side_effects=True, vmem_limit_bytes=60 << 20
        ),
    )(aggregate, lane_tiles(operator), lane_tiles(vectors))
    within = within.reshape(3, AGGS, 32, AGGS, LANES).transpose(0, 1, 3, 2, 4)
    cross = cross.reshape(4, 32, AGGS, LANES).transpose(0, 2, 1, 3)
    return (
        within.reshape(1, 1, 3, AGGS, AGGS, NULLCOLS * NULLCOLS),
        cross.reshape(1, 1, 4, AGGS, NULLCOLS * NULLCOLS),
    )


def solution(mesh):
    return jax.shard_map(
        per_device,
        mesh=mesh,
        in_specs=(P("ta", "sa", None, None), P("ta", "sa", None, None), P()),
        out_specs=(P("ta", "sa", None, None, None, None), P("ta", "sa", None, None, None)),
        check_vma=False,
    )
```

time: 169 us -> 50.1 us (0.30)
  the two profiles are of different devices: /device:TPU:120 before, /device:TPU:7 now
where the time goes in v1:
time: 50.1 us; the launch traced here: 50 us
  Pallas kernels  46.1 us (92%)
  local copies, waits for them, and re-layouts  3.18 us (6%)
  between operations  0.64 us (1%)
    pallas_call x1, Pallas kernels, per_device(): pl.pallas_call(kernel, out_shape=(jax.ShapeDtypeStruct((3 * AGGS, 64, LAN...  46.1 us
    unnamed x2, local copies, waits for them, and re-layouts  3.18 us

profile of v1, /device:TPU:7, one launch (start us, length us, event | category | flops | bytes accessed | tf_op | source)
XLA Modules:
  0.0 50.0 jit_solution(1937328557663675364)
XLA Ops:
  0.6 46.1 %shard_map.50 = (f32[6,64,128]{2,1,0:T(8,128)}, f32[4,64,128]{2,1,0:T(8,128)}) custom-call(s32[6]{0:T(128)} %agg_ref.1, bf16[2,6,1296,128]{3,2,1,0:T(8,128)(2,1)} %bitcast.20, bf16[2,6,96,128]{3,2,1,0:T(8,128)(2,1)} %bitcast.21), custom_call_target="tpu_custom_call" | custom-call | tf_op jit(solution)/shard_map/pallas_call | solution.py:332
  46.8 1.6 %copy.11 = f32[1,1,3,2,2,4096]{5,4,3,2,1,0:T(2,128)} copy(f32[1,1,3,2,2,4096]{5,4,3,2,1,0:T(2,128)} %bitcast.22) | data formatting | bytes 393216
  48.4 1.6 %copy.12 = f32[1,1,4,2,4096]{4,3,2,1,0:T(2,128)} copy(f32[1,1,4,2,4096]{4,3,2,1,0:T(2,128)} %bitcast.23) | data formatting | bytes 262144

commit v2 on v1

v2 whole, which is shorter than its diff:
```python
import jax
import jax.numpy as jnp
from jax import lax
from jax.experimental import pallas as pl
from jax.experimental.pallas import tpu as pltpu
from jax.sharding import PartitionSpec as P

BLOCK = 96
NULLCOLS = 64
LX = 2
LY = 3
XSPLIT = 8
AGGS = 2
SITES = LX * LY
HOPS = 9
LANES = 128
GROUPS = BLOCK // 4
MESH = pl.DeviceIdType.MESH
F32 = jnp.float32
BF16 = jnp.bfloat16


def lane_half(rows):
    return lax.broadcasted_iota(jnp.int32, (rows, LANES), 1) < NULLCOLS


def swap(value):
    return pltpu.roll(value, NULLCOLS, 1)


def block_weights(packed):
    low = lane_half(BLOCK)
    wide = packed.astype(F32)
    turned = swap(wide)
    zero = jnp.zeros_like(wide)
    gap = jnp.zeros((2 * LANES - 2 * BLOCK, LANES), BF16)
    out = []
    for first, second in ((wide, turned), (turned, wide)):
        left = jnp.where(low, first, zero).astype(BF16)
        right = jnp.where(low, zero, second).astype(BF16)
        out.append((jnp.concatenate([left, right, gap], axis=0), jnp.concatenate([gap, left, right], axis=0)))
    return out


def kernel(
    agg_hbm, op_hbm, vec_hbm, within_ref, cross_ref,
    agg_ref, op_v, vec_v, op_f, vec_f, mix, pack_t, pack_x, halo_t, halo_z, halo_x, img, turn, left,
    part, pt_out, pt_in, pz_out, pz_in, load_sem, send_sem, recv_sem,
):
    nt = lax.axis_size("ta")
    ns = lax.axis_size("sa")
    ti = lax.axis_index("ta")
    sj = lax.axis_index("sa")
    slab = sj // XSPLIT * XSPLIT
    xi = sj % XSPLIT
    t_up = ((ti + 1) % nt, sj)
    t_down = ((ti + nt - 1) % nt, sj)
    z_up = (ti, (sj + XSPLIT) % ns)
    z_down = (ti, (sj + ns - XSPLIT) % ns)
    x_up = (ti, slab + (xi + 1) % XSPLIT)
    x_down = (ti, slab + (xi + XSPLIT - 1) % XSPLIT)

    barrier = pltpu.get_barrier_semaphore()
    for there in (t_up, t_down, z_up, z_down, x_up, x_down):
        pl.semaphore_signal(barrier, inc=1, device_id=there, device_id_type=MESH)
    vec_load = pltpu.make_async_copy(vec_hbm, vec_v, load_sem.at[2])
    vec_load.start()
    agg_load = pltpu.make_async_copy(agg_hbm, agg_ref, load_sem.at[3])
    agg_load.start()
    op_loads = [pltpu.make_async_copy(op_hbm.at[t], op_v.at[t], load_sem.at[t]) for t in range(2)]
    for load in op_loads:
        load.start()

    def remote(index, src, dst, there):
        return pltpu.make_async_remote_copy(
            src_ref=src, dst_ref=dst, send_sem=send_sem.at[index], recv_sem=recv_sem.at[index],
            device_id=there, device_id_type=MESH,
        )

    vec_load.wait()
    low48 = lane_half(48)

    def vec_wide(ts, carry):
        vec_f[ts] = vec_v[ts // SITES, ts % SITES].astype(F32)
        return carry

    lax.fori_loop(0, 2 * SITES, vec_wide, 0, unroll=4)

    def paired(first, second, z, spare):
        v0 = vec_f[first, pl.ds(z, 48, stride=2), :]
        v1 = vec_f[second, pl.ds(z, 48, stride=2), :]
        mix[spare, pl.ds(0, 48, stride=2), :] = jnp.where(low48, v0, swap(v1))
        mix[spare, pl.ds(1, 48, stride=2), :] = jnp.where(low48, swap(v0), v1)
        return mix[spare].astype(BF16)

    def pair_times(z):
        def one(s, carry):
            pack_t[z, s] = paired(s, SITES + s, z, s % 4)
            return carry

        lax.fori_loop(0, SITES, one, 0, unroll=True)

    def pair_sites(z):
        def one(tx, carry):
            t, x2 = tx // LY, tx % LY
            pack_x[z, t, x2] = paired(t * SITES + x2, t * SITES + LY + x2, z, tx % 4)
            return carry

        lax.fori_loop(0, SITES, one, 0, unroll=True)

    x_face, t_face = {}, {}
    for z in range(2):
        x_face[z] = (
            remote(2 * z, pack_t.at[z, LY:SITES], halo_x.at[0, z], x_up),
            remote(2 * z + 1, pack_t.at[z, 0:LY], halo_x.at[1, z], x_down),
        )
        t_face[z] = (
            remote(4 + 2 * z, pack_x.at[z, 1], halo_t.at[0, z], t_up),
            remote(5 + 2 * z, pack_x.at[z, 0], halo_t.at[1, z], t_down),
        )
    z_face = (
        remote(8, pack_x.at[1], halo_z.at[0], z_up),
        remote(9, pack_x.at[0], halo_z.at[1], z_down),
    )
    cuts = (slice(0, 4), slice(4, 12), slice(12, 16))
    pt = {
        (1, c): remote(10 + c, pt_out.at[1, cuts[c]], pt_in.at[1, cuts[c]], t_up) for c in range(3)
    }
    pt[0, 0] = remote(13, pt_out.at[0, 0:4], pt_in.at[0, 0:4], t_up)
    pt[0, 1] = remote(14, pt_out.at[0, 4:16], pt_in.at[0, 4:16], t_up)
    pz_cuts = (slice(0, 4), slice(4, 12), slice(12, 18))
    pz = [remote(15 + c, pz_out.at[pz_cuts[c]], pz_in.at[pz_cuts[c]], z_up) for c in range(3)]

    pair_times(1)
    pl.semaphore_wait(barrier, 6)
    for face in x_face[1]:
        face.start()
    pair_sites(0)
    z_face[1].start()
    pair_sites(1)
    z_face[0].start()
    for face in t_face[1]:
        face.start()
    pair_times(0)
    for face in (*x_face[0], *t_face[0]):
        face.start()

    for t in (1, 0):
        op_loads[t].wait()

        def widen(s, carry):
            op_f[t * SITES + s] = op_v[t, s].astype(F32)
            return carry

        lax.fori_loop(0, SITES, widen, 0)

    def rows_of(ts, z, hop):
        return [
            op_f[ts, pl.ds(hop * 144 + 2 * v + z, GROUPS, stride=6), :] for v in range(3)
        ]

    def images(users, weights):
        parts = [rows_of(ts, z, hop) for ts, z, hop in users]
        tiles = [jnp.concatenate([part[v] for part in parts], axis=0).astype(BF16) for v in range(3)]
        for half in range(2):
            got = jnp.dot(
                jnp.concatenate([tiles[half], tiles[half + 1]], axis=1), weights[half],
                preferred_element_type=F32,
            ).astype(BF16).astype(F32)
            for i, (ts, z, hop) in enumerate(users):
                img[ts * 2 + z, hop, :, LANES * half:LANES * (half + 1)] = got[GROUPS * i:GROUPS * (i + 1)]

    def local(z):
        def one(t, carry):
            for x2 in range(LY):
                here = block_weights(pack_x[z, t, x2])
                beside = block_weights(pack_x[1 - z, t, x2])
                for x1 in range(LX):
                    s = x1 * LY + x2
                    users = (
                        (t * SITES + s, z, 0),
                        ((1 - t) * SITES + s, z, 2 - t),
                        (t * SITES + (1 - x1) * LY + x2, z, 5 if x1 == 1 else 6),
                        (t * SITES + x1 * LY + (x2 + 2) % LY, z, 7),
                        (t * SITES + x1 * LY + (x2 + 1) % LY, z, 8),
                    )
                    images(users, here[x1])
                    images(((t * SITES + s, z, 3 + z),), beside[x1])
            return carry

        lax.fori_loop(0, 2, one, 0, unroll=True)

    column = lax.broadcasted_iota(jnp.int32, (1, SITES * GROUPS), 1)
    agg_load.wait()
    member = [agg_ref[s].astype(F32) for s in range(SITES)]
    others = [1.0 - m for m in member]
    weight_of = (others, member)
    mask = []
    for a in range(AGGS):
        row = jnp.zeros((1, SITES * GROUPS), F32)
        for s in range(SITES):
            inside = jnp.logical_and(column >= s * GROUPS, column < (s + 1) * GROUPS)
            row = row + jnp.where(inside, weight_of[a][s], 0.0)
        mask.append(row)
    pad = jnp.zeros((2 * LANES - SITES * GROUPS, LANES), F32)

    def left_side(t, z):
        tz = t * 2 + z
        for h in range(2):
            blocks = [vec_f[t * SITES + s, pl.ds(2 * h + z, GROUPS, stride=4), :] for s in range(SITES)]
            spare = t * 2 + h
            turned = jnp.transpose(jnp.concatenate(blocks + [pad], axis=0))
            for side in range(2):
                turn[spare, side] = turned[:, LANES * side:LANES * (side + 1)]
            for low in range(2):
                for par in range(2):
                    rows = jnp.concatenate(
                        [turn[spare, side, pl.ds(low * NULLCOLS + par, 32, stride=2), :] for side in range(2)],
                        axis=1,
                    )[:, :SITES * GROUPS]
                    for a in range(AGGS):
                        at = ((a * 2 + low) * 2 + par) * 32
                        left[tz, h, at:at + 32, :] = (rows * mask[a]).astype(BF16)

    def t_side(t, z):
        def one(x2, carry):
            both = block_weights(halo_t[t, z, x2])
            for x1 in range(LX):
                images(((t * SITES + x1 * LY + x2, z, 2 - t),), both[x1])
            return carry

        lax.fori_loop(0, LY, one, 0, unroll=True)

    def z_side(t, z):
        def one(x2, carry):
            both = block_weights(halo_z[z, t, x2])
            for x1 in range(LX):
                images(((t * SITES + x1 * LY + x2, z, 4 - z),), both[x1])
            return carry

        lax.fori_loop(0, LY, one, 0, unroll=True)

    def x_side(z):
        def one(s, carry):
            x1, x2 = s // LY, s % LY
            both = block_weights(halo_x[x1, z, x2])
            for t in range(2):
                images(((t * SITES + s, z, 6 - x1),), both[t])
            return carry

        lax.fori_loop(0, SITES, one, 0, unroll=True)

    low32 = lane_half(32)

    def product(t, z, n, keep):
        tz = t * 2 + z
        t_stay, t_leave = (1, 2) if t == 1 else (2, 1)
        z_stay, z_leave = (3, 4) if z == 1 else (4, 3)
        right = []
        for h in range(2):
            cut = slice(LANES * h, LANES * (h + 1))
            columns = [[], []]
            blank = jnp.zeros((GROUPS, LANES), F32)
            for s in range(SITES):
                x1, x2 = s // LY, s % LY
                at = (t * SITES + s) * 2 + z
                take = lambda hop: img[at, hop, :, cut]
                x_stay, x_leave = (6, 5) if x1 == 1 else (5, 6)
                across = (1 - x1) * LY + x2
                up, down = x1 * LY + (x2 + 1) % LY, x1 * LY + (x2 + 2) % LY
                if n == 0:
                    same = take(0) + take(t_stay) + take(z_stay)
                    inner, plus, minus = take(x_stay), take(7), take(8)
                    for b in range(AGGS):
                        w = weight_of[b]
                        columns[b].append(w[s] * same + w[across] * inner + w[up] * plus + w[down] * minus)
                elif n == 3:
                    columns[0].append(take(t_leave))
                    columns[1].append(take(z_leave))
                else:
                    outer = take(x_leave) if x1 == 2 - n else None
                    for b in range(AGGS):
                        columns[b].append(blank if outer is None else weight_of[b][across] * outer)
            right.append(
                jnp.concatenate([jnp.concatenate(c, axis=0).astype(BF16) for c in columns], axis=1)
            )
        for a in range(AGGS):
            rows = slice(LANES * a, LANES * (a + 1))
            got = jnp.dot(left[tz, 0, rows, :], right[0], preferred_element_type=F32)
            got = got + jnp.dot(left[tz, 1, rows, :], right[1], preferred_element_type=F32)
            for c in range(2):
                cut = got[:, LANES * c:LANES * (c + 1)]
                value = jnp.where(low32, cut[0:32] + swap(cut[64:96]), swap(cut[32:64]) + cut[96:128])
                keep(n * 4 + a * 2 + c if n < 3 else 12 + c * 2 + a, value)

    def to_send(z):
        def keep(block, value):
            pt_out[z, block] = value.astype(BF16)

        return keep

    def to_keep(z):
        def keep(block, value):
            part[z, block] = value

        return keep

    left_side(1, 1)
    left_side(0, 1)
    local(1)
    product(1, 1, 3, to_send(1))
    pt[1, 2].start()
    product(0, 1, 3, to_keep(1))
    for face in x_face[1]:
        face.wait_recv()
    x_side(1)
    for n in (1, 2):
        product(1, 1, n, to_send(1))
    pt[1, 1].start()
    for n in (1, 2):
        product(0, 1, n, to_keep(1))
    pt[1, 2].wait_recv()
    for a in range(AGGS):
        pz_out[12 + a] = part[1, 12 + a].astype(BF16)
        pz_out[14 + a] = pt_in[1, 12 + a]
        pz_out[16 + a] = (part[1, 14 + a] + pt_in[1, 14 + a].astype(F32)).astype(BF16)
    pz[2].start()
    for face in t_face[1]:
        face.wait_recv()
    t_side(1, 1)
    z_face[1].wait_recv()
    z_side(1, 1)
    product(1, 1, 0, to_send(1))
    pt[1, 0].start()
    t_side(0, 1)
    z_side(0, 1)
    product(0, 1, 0, to_keep(1))
    pt[1, 1].wait_recv()
    for block in range(4, 12):
        pz_out[block] = (part[1, block] + pt_in[1, block].astype(F32)).astype(BF16)
    pz[1].start()
    pt[1, 0].wait_recv()
    for block in range(4):
        pz_out[block] = (part[1, block] + pt_in[1, block].astype(F32)).astype(BF16)
    pz[0].start()

    left_side(1, 0)
    left_side(0, 0)
    local(0)
    product(1, 0, 3, to_send(0))
    product(0, 0, 3, to_keep(0))
    for face in x_face[0]:
        face.wait_recv()
    x_side(0)
    for n in (1, 2):
        product(1, 0, n, to_send(0))
    pt[0, 1].start()
    for n in (1, 2):
        product(0, 0, n, to_keep(0))
    for face in t_face[0]:
        face.wait_recv()
    t_side(1, 0)
    t_side(0, 0)
    z_face[0].wait_recv()
    z_side(1, 0)
    product(1, 0, 0, to_send(0))
    pt[0, 0].start()
    z_side(0, 0)
    product(0, 0, 0, to_keep(0))
    pt[0, 1].wait_recv()
    for block in (*range(4, 12), 14, 15):
        part[0, block] = part[0, block] + pt_in[0, block].astype(F32)
    pz[2].wait_recv()
    for a in range(AGGS):
        cross_ref[0, pl.ds(a, 32, stride=2), :] = part[0, 12 + a] + pz_in[12 + a].astype(F32)
        cross_ref[1, pl.ds(a, 32, stride=2), :] = pt_in[0, 12 + a].astype(F32) + pz_in[14 + a].astype(F32)
        cross_ref[2, pl.ds(a, 32, stride=2), :] = part[0, 14 + a]
        cross_ref[3, pl.ds(a, 32, stride=2), :] = pz_in[16 + a].astype(F32)

    def finish(blocks):
        for block in blocks:
            within_ref[block // 2, pl.ds(block % 2, 32, stride=2), :] = part[0, block] + pz_in[block].astype(F32)

    pz[1].wait_recv()
    finish(range(4, 12))
    pt[0, 0].wait_recv()
    for block in range(4):
        part[0, block] = part[0, block] + pt_in[0, block].astype(F32)
    pz[0].wait_recv()
    finish(range(4))
    for copy in (*x_face[0], *x_face[1], *t_face[0], *t_face[1], *z_face, *pt.values(), *pz):
        copy.wait_send()


def lane_tiles(field):
    time, depth, sites, length = field.shape
    split = field.reshape(time, depth, sites, length // LANES, LANES)
    return split.transpose(0, 2, 3, 1, 4).reshape(time, sites, length // LANES * depth, LANES)


def per_device(operator, vectors, aggregate):
    op_rows = HOPS * BLOCK * BLOCK // LANES * 2
    vec_rows = BLOCK * NULLCOLS // LANES * 2
    within, cross = pl.pallas_call(
        kernel,
        out_shape=(
            jax.ShapeDtypeStruct((3 * AGGS, 64, LANES), F32),
            jax.ShapeDtypeStruct((4, 64, LANES), F32),
        ),
        in_specs=[
            pl.BlockSpec(memory_space=pltpu.HBM),
            pl.BlockSpec(memory_space=pltpu.HBM),
            pl.BlockSpec(memory_space=pltpu.HBM),
        ],
        out_specs=[pl.BlockSpec(memory_space=pltpu.VMEM)] * 2,
        scratch_shapes=[
            pltpu.SMEM((SITES,), jnp.int32),
            pltpu.VMEM((2, SITES, op_rows, LANES), BF16),
            pltpu.VMEM((2, SITES, vec_rows, LANES), BF16),
            pltpu.VMEM((2 * SITES, op_rows, LANES), F32),
            pltpu.VMEM((2 * SITES, vec_rows, LANES), F32),
            pltpu.VMEM((4, BLOCK, LANES), F32),
            pltpu.VMEM((2, SITES, BLOCK, LANES), BF16),
            pltpu.VMEM((2, 2, LY, BLOCK, LANES), BF16),
            pltpu.VMEM((2, 2, LY, BLOCK, LANES), BF16),
            pltpu.VMEM((2, 2, LY, BLOCK, LANES), BF16),
            pltpu.VMEM((2, 2, LY, BLOCK, LANES), BF16),
            pltpu.VMEM((4 * SITES, HOPS, GROUPS, 2 * LANES), F32),
            pltpu.VMEM((4, 2, LANES, LANES), F32),
            pltpu.VMEM((4, 2, 2 * LANES, SITES * GROUPS), BF16),
            pltpu.VMEM((2, 16, 32, LANES), F32),
            pltpu.VMEM((2, 16, 32, LANES), BF16),
            pltpu.VMEM((2, 16, 32, LANES), BF16),
            pltpu.VMEM((18, 32, LANES), BF16),
            pltpu.VMEM((18, 32, LANES), BF16),
            pltpu.SemaphoreType.DMA((4,)),
            pltpu.SemaphoreType.DMA((18,)),
            pltpu.SemaphoreType.DMA((18,)),
        ],
        compiler_params=pltpu.CompilerParams(
            collective_id=0, has_side_effects=True, vmem_limit_bytes=40 << 20
        ),
    )(
        pltpu.with_memory_space_constraint(aggregate, pltpu.HBM),
        pltpu.with_memory_space_constraint(lane_tiles(operator), pltpu.HBM),
        pltpu.with_memory_space_constraint(lane_tiles(vectors), pltpu.HBM),
    )
    within = within.reshape(3, AGGS, 32, AGGS, LANES).transpose(0, 1, 3, 2, 4)
    cross = cross.reshape(4, 32, AGGS, LANES).transpose(0, 2, 1, 3)
    return (
        within.reshape(1, 1, 3, AGGS, AGGS, NULLCOLS * NULLCOLS),
        cross.reshape(1, 1, 4, AGGS, NULLCOLS * NULLCOLS),
    )


def solution(mesh):
    return jax.shard_map(
        per_device,
        mesh=mesh,
        in_specs=(P("ta", "sa", None, None), P("ta", "sa", None, None), P()),
        out_specs=(P("ta", "sa", None, None, None, None), P("ta", "sa", None, None, None)),
        check_vma=False,
    )
```

time: 50.1 us -> 37.1 us (0.74)
  the two profiles are of different devices: /device:TPU:7 before, /device:TPU:16 now
where the time goes in v2:
time: 37.1 us; the launch traced here: 37 us
  Pallas kernels  35 us (94%)
  local copies, waits for them, and re-layouts  1.33 us (4%)
  between operations  0.64 us (2%)
    pallas_call x1, Pallas kernels, per_device(): pl.pallas_call(kernel, out_shape=(jax.ShapeDtypeStruct((3 * AGGS, 64, LAN...  35 us
    unnamed x2, local copies, waits for them, and re-layouts  1.33 us

profile of v2, /device:TPU:16, one launch (start us, length us, event | category | flops | bytes accessed | tf_op | source)
XLA Modules:
  0.0 37.0 jit_solution(3804352438867892728)
XLA Ops:
  0.6 35.0 %shard_map.50 = (f32[6,64,128]{2,1,0:T(8,128)S(1)}, f32[4,64,128]{2,1,0:T(8,128)S(1)}) custom-call(s32[6]{0:T(128)} %agg_hbm.1, bf16[2,6,1296,128]{3,2,1,0:T(8,128)(2,1)} %bitcast.22, bf16[2,6,96,128]{3,2,1,0:T(8,128)(2,1)} %bitcast.23), custom_call_target="tpu_custom_call" | custom-call | tf_op jit(solution)/shard_map/pallas_call | solution.py:404
  35.6 0.7 %copy.11 = f32[1,1,3,2,2,4096]{5,4,3,2,1,0:T(2,128)} copy(f32[1,1,3,2,2,4096]{5,4,3,2,1,0:T(2,128)S(1)} %bitcast.20) | data formatting | bytes 393216
  36.3 0.7 %copy.12 = f32[1,1,4,2,4096]{4,3,2,1,0:T(2,128)} copy(f32[1,1,4,2,4096]{4,3,2,1,0:T(2,128)S(1)} %bitcast.21) | data formatting | bytes 262144
